TPU v7x, 32 devices: a whole 2x2x4 slice. The times are simulated.
32 devices in a mesh: row: 8 (over z, y), col: 4 (over x, core).
Axes of the slice: x: 2, y: 2, z: 4, core: 2. Of those that a mesh axis runs over, the one named last changes fastest.
Arguments:
- hidden: bfloat16 [64, 4096], P('row'), may hold values from -6 to 6
- queries: bfloat16 [64, 64, 128], P(('row', 'col')), may hold values from -6 to 6
- keys: bfloat16 [64, 4, 64, 128], P(('row', 'col')), may hold values from -6 to 6
- values: bfloat16 [64, 4, 64, 128], P(('row', 'col')), may hold values from -12 to 12
- out_proj: bfloat16 [8192, 4096], P('col'), may hold values from -0.0625 to 0.0625
- norm_gain: float32 [4096], replicated, may hold values from 0.4 to 1.6
- routes: int32 [64, 8], P('row'), may hold values from 0 to 127, all different within a row; in each aligned block of 8 rows (0 to 7, 8 to 15, ...) at most 8 rows name the same one
- route_probs: float32 [64, 8], P('row'), may hold values from 0.05 to 1
- w_gate: bfloat16 [4096, 131072], P(None, ('row', 'col')), may hold values from -0.09375 to 0.09375
- w_up: bfloat16 [4096, 131072], P(None, ('row', 'col')), may hold values from -0.09375 to 0.09375
- w_down: bfloat16 [131072, 4096], P(('row', 'col')), may hold values from -0.1875 to 0.1875
Outputs:
- updated: bfloat16 [64, 4096], P(('row', 'col'))
Inputs may be any that keep to these rules, and one draw needn't show every extreme that they name: `routes`: each row names 8 different experts. In each aligned block of 8 rows (the requests of one index of row) no expert is named by more than 8 rows.
All inputs are finite; a program needn't handle non-finite values.
Results may differ from a plain program's by a relative error of at most 0.017.
Values may be sent and summed in bfloat16 or wider, within the bound.
A program may use at most 256 MiB of HBM per device.

v0:
```python
import math

import jax
import jax.numpy as jnp
from jax import lax
from jax.sharding import PartitionSpec as P

FF = 1024
CAP = 8


def normalize(resid, norm_gain):
    mean_square = jnp.mean(resid * resid, axis=-1, keepdims=True)
    return (resid * lax.rsqrt(mean_square + 1e-06) * norm_gain).astype(jnp.bfloat16)


def shards(
    hidden, queries, keys, values, out_proj, norm_gain, routes, route_probs, w_gate, w_up, w_down
):
    row_count = lax.axis_size("row")
    col_count = lax.axis_size("col")
    col_id = lax.axis_index("col")
    tok_dev = queries.shape[0]
    heads = queries.shape[1]
    head_dim = queries.shape[2]
    kv_heads = keys.shape[1]
    group = heads // kv_heads
    d_model = w_gate.shape[0]
    hid_dev = w_gate.shape[1]
    grouped = queries.reshape(tok_dev, kv_heads, group, head_dim)
    scores = jnp.einsum(
        "tgqd,tgpd->tgqp", grouped, keys, preferred_element_type=jnp.float32
    ) / math.sqrt(head_dim)
    attn_weights = jax.nn.softmax(scores, axis=-1).astype(jnp.bfloat16)
    context = jnp.einsum(
        "tgqp,tgpd->tgqd", attn_weights, values, preferred_element_type=jnp.float32
    )
    context = context.astype(jnp.bfloat16).reshape(tok_dev, heads * head_dim)
    head_rows = lax.all_to_all(context, "col", split_axis=1, concat_axis=0, tiled=True)
    partial_sum = jnp.dot(head_rows, out_proj, preferred_element_type=jnp.float32)
    attn = lax.psum(partial_sum.astype(jnp.bfloat16), "col").astype(jnp.float32)
    row_resid = hidden.astype(jnp.float32) + attn
    normed = normalize(row_resid, norm_gain)
    resid = lax.dynamic_slice_in_dim(row_resid, col_id * tok_dev, tok_dev, 0)
    route_weight = (route_probs / jnp.sum(route_probs, axis=-1, keepdims=True)).astype(jnp.bfloat16)
    exp_local = max(1, hid_dev // FF)
    slice_width = hid_dev // exp_local
    dest_rows = jnp.arange(row_count, dtype=jnp.int32)
    experts_at = (dest_rows[:, None] * col_count + col_id) * hid_dev // FF
    experts_at = experts_at + jnp.arange(exp_local, dtype=jnp.int32)[None, :]
    match = routes[:, :, None, None] == experts_at[None, None, :, :]
    hits = jnp.any(match, axis=1).astype(jnp.int32)
    chosen = jnp.sum(
        jnp.where(match, route_weight[:, :, None, None], jnp.zeros((), jnp.bfloat16)), axis=1
    )
    before = jnp.cumsum(hits, axis=0) - hits
    hits_t = jnp.transpose(hits, (1, 2, 0))
    before_t = jnp.transpose(before, (1, 2, 0))
    slot_ids = jnp.arange(CAP, dtype=jnp.int32)
    place = (hits_t[:, :, None, :] == 1) & (
        before_t[:, :, None, :] == slot_ids[None, None, :, None]
    )
    place = place.astype(jnp.bfloat16)
    gate_local = w_gate.reshape(d_model, exp_local, slice_width)
    up_local = w_up.reshape(d_model, exp_local, slice_width)
    down_local = w_down.reshape(exp_local, slice_width, d_model)
    scaled = place * jnp.transpose(chosen, (1, 2, 0))[:, :, None, :]
    outgoing = jnp.einsum(
        "rjkt,td->rjkd", place, normed, preferred_element_type=jnp.float32
    ).astype(jnp.bfloat16)
    arrived = lax.all_to_all(outgoing, "row", split_axis=0, concat_axis=0, tiled=True)
    gate = jnp.einsum("qjkd,dje->qjke", arrived, gate_local, preferred_element_type=jnp.float32)
    upward = jnp.einsum("qjkd,dje->qjke", arrived, up_local, preferred_element_type=jnp.float32)
    act = (jax.nn.silu(gate) * upward).astype(jnp.bfloat16)
    returned = lax.all_to_all(
        jnp.einsum("qjke,jed->qjkd", act, down_local, preferred_element_type=jnp.float32).astype(
            jnp.bfloat16
        ),
        "row",
        split_axis=0,
        concat_axis=0,
        tiled=True,
    )
    mixture = lax.psum_scatter(
        jnp.einsum("rjkt,rjkd->td", scaled, returned, preferred_element_type=jnp.float32).astype(
            jnp.bfloat16
        ),
        "col",
        scatter_dimension=0,
        tiled=True,
    ).astype(jnp.float32)
    return (resid + mixture).astype(jnp.bfloat16)


def solution(mesh):
    return jax.shard_map(
        shards,
        mesh=mesh,
        in_specs=(
            P("row", None),
            P(("row", "col"), None, None),
            P(("row", "col"), None, None, None),
            P(("row", "col"), None, None, None),
            P("col", None),
            P(),
            P("row", None),
            P("row", None),
            P(None, ("row", "col")),
            P(None, ("row", "col")),
            P(("row", "col"), None),
        ),
        out_specs=P(("row", "col"), None),
        check_vma=False,
    )
```

profile of v0, /device:TPU:0, one launch (start us, length us, event | category | flops | bytes accessed | tf_op | source)
XLA Modules:
  0.0 375.0 jit_solution(3656178389710261590)
XLA Ops:
  6.5 1.1 convolution_multiply_fusion
  7.7 0.2 fusion.43
  7.9 0.3 convolution_convert_fusion.3
  8.2 0.6 copy.28
  8.8 4.2 %all-to-all-start = ((bf16[2,4,2048]{2,0,1:T(2,128)(2,1)}), bf16[2,4,2048]{2,0,1:T(2,128)(2,1)S(1)}, u32[]{:S(2)}, u32[]{:S(2)}) async-start(bf16[2,4,2048]{2,0,1:T(2,128)(2,1)} %copy.28), calls=%async_computation | async-start | bytes 65536 | tf_op jit(solution)/shard_map/all_to_all | solution.py:39
  13.1 0.8 compare_reduce_fusion
  13.9 3.0 all-to-all-done
  17.0 0.0 copy-start.2
  17.0 8.7 %convolution_convert_fusion.2 = bf16[8,4096]{1,0:T(8,128)(2,1)} fusion(bf16[8,2048]{1,0:T(8,128)(2,1)S(1)} %all_to_all.23, bf16[2048,4096]{1,0:T(8,128)(2,1)} %param.15), kind=kOutput, calls=%fused_computation.10 | convolution fusion | flops 134250496 | bytes 16875520 | tf_op jit(solution)/shard_map/dot_general | solution.py:40
  25.7 0.0 all-reduce.4.cloned.1.call-update
  25.8 0.2 copy.32
  26.0 31.8 %all-reduce.4.cloned.1.call-done = bf16[8,4096]{1,0:T(8,128)(2,1)} async-done(((bf16[8,4096]{1,0:T(8,128)(2,1)}), bf16[8,4096]{1,0:T(8,128)(2,1)}) %all-reduce.4.cloned.1.call-update) | async-done | bytes 65552 | tf_op jit(solution)/shard_map/psum | solution.py:41
  57.8 1.0 multiply_reduce_fusion
  58.8 2.9 convolution_convert_fusion.1
  61.7 5.5 %all-to-all-start.1 = ((bf16[8,4,8,4096]{3,2,1,0:T(8,128)(2,1)}), bf16[8,4,8,4096]{3,2,1,0:T(8,128)(2,1)S(1)}, u32[]{:S(2)}, u32[]{:S(2)}) async-start(bf16[8,4,8,4096]{3,2,1,0:T(8,128)(2,1)} %convolution_convert_fusion.1), calls=%async_computation.1 | async-start | bytes 4194304 | tf_op jit(solution)/shard_map/all_to_all | solution.py:71
  67.2 54.6 %reshape.97 = bf16[4096,4,1024]{2,1,0:T(4,128)(2,1)} reshape(bf16[4096,4096]{1,0:T(8,128)(2,1)} %param.19) | data formatting | bytes 67108864 | tf_op jit(solution)/shard_map/reshape | solution.py:64
  121.8 54.6 %reshape.98 = bf16[4096,4,1024]{2,1,0:T(4,128)(2,1)} reshape(bf16[4096,4096]{1,0:T(8,128)(2,1)} %param.20) | data formatting | bytes 67108864 | tf_op jit(solution)/shard_map/reshape | solution.py:65
  176.3 39.1 %fusion.10 = f32[8,4,8,1024]{3,2,0,1:T(8,128)} fusion(bf16[4096,4,1024,1]{2,1,0,3:T(4,128)(2,1)} %bitcast.47, bf16[8,4,8,4096]{3,2,1,0:T(8,128)(2,1)S(1)} %all-to-all-done.1), kind=kOutput, calls=%fused_computation.14 | convolution fusion | flops 2147483648 | bytes 36700160 | tf_op jit(solution)/shard_map/qjkd,dje->qjke/dot_general | solution.py:72
  215.5 49.9 %multiply_convert_fusion = bf16[8,4,8,1024]{3,2,0,1:T(8,128)(2,1)S(1)} fusion(f32[8,4,8,1024]{3,2,0,1:T(8,128)} %fusion.10, bf16[4096,4,1024,1]{2,1,0,3:T(4,128)(2,1)} %bitcast.46, bf16[8,4,8,4096]{3,2,1,0:T(8,128)(2,1)S(1)} %all-to-all-done.1), kind=kOutput, calls=%fused_computation.22 | convolution fusion | flops 2149056512 | bytes 37224448 | tf_op jit(solution)/shard_map/qjkd,dje->qjke/dot_general | solution.py:73
  265.4 13.8 %fusion.5 = bf16[8,4,8,4096]{3,0,2,1:T(8,128)(2,1)S(1)} fusion(bf16[4,1024,4096,1]{2,1,3,0:T(8,128)(2,1)} %bitcast.45, bf16[8,4,8,1024]{3,2,0,1:T(8,128)(2,1)S(1)} %multiply_convert_fusion), kind=kOutput, calls=%fused_computation.7 | convolution fusion | flops 2148532224 | bytes 36175872 | tf_op jit(solution)/shard_map/qjke,jed->qjkd/dot_general | solution.py:76
  279.2 2.5 copy.38
  281.7 6.1 %all-to-all-start.2 = ((bf16[8,4,8,4096]{3,2,1,0:T(8,128)(2,1)}), bf16[8,4,8,4096]{3,2,1,0:T(8,128)(2,1)S(1)}, u32[]{:S(2)}, u32[]{:S(2)}) async-start(bf16[8,4,8,4096]{3,2,1,0:T(8,128)(2,1)} %copy.38), calls=%async_computation.2 | async-start | bytes 4194304 | tf_op jit(solution)/shard_map/all_to_all | solution.py:75
  287.9 0.0 all-reduce.6.cloned.1.call-start
  287.9 0.1 reduce_sum.40
  288.0 0.1 divide_convert_fusion.2
  288.1 0.1 fusion.31
  288.3 46.3 %all-to-all-done.2 = bf16[8,4,8,4096]{3,2,1,0:T(8,128)(2,1)S(1)} async-done(((bf16[8,4,8,4096]{3,2,1,0:T(8,128)(2,1)}), bf16[8,4,8,4096]{3,2,1,0:T(8,128)(2,1)S(1)}, u32[]{:S(2)}, u32[]{:S(2)}) %all-to-all-start.2) | async-done | bytes 2097184 | tf_op jit(solution)/shard_map/all_to_all | solution.py:75
  334.6 2.3 fusion.6
  336.9 0.0 all-reduce.6.cloned.1.call-update
  336.9 0.6 dynamic-slice
  338.2 28.3 %all-reduce.6.cloned.1.call-done = bf16[8,4096]{1,0:T(8,128)(2,1)} async-done(((bf16[8,4096]{1,0:T(8,128)(2,1)}), bf16[8,4096]{1,0:T(8,128)(2,1)}) %all-reduce.6.cloned.1.call-update) | async-done | bytes 65552
  366.5 1.5 add_convert_fusion
  (26 shorter events, 0.2 us)
Async XLA Ops:
  6.5 1.3 copy-start
  8.8 8.2 %all-to-all-start = ((bf16[2,4,2048]{2,0,1:T(2,128)(2,1)}), bf16[2,4,2048]{2,0,1:T(2,128)(2,1)S(1)}, u32[]{:S(2)}, u32[]{:S(2)}) async-start(bf16[2,4,2048]{2,0,1:T(2,128)(2,1)} %copy.28), calls=%async_computation | async-start | bytes 65536 | tf_op jit(solution)/shard_map/all_to_all | solution.py:39
  13.0 44.7 %all-reduce.4.cloned.1.call-start = ((), (), s32[]{:S(2)}) async-start(), calls=%async_computation.3 | async-start | bytes 131072 | tf_op jit(solution)/shard_map/psum | solution.py:41
  17.0 40.8 %copy-start.2 = (bf16[8,4096]{1,0:T(8,128)(2,1)S(1)}, bf16[8,4096]{1,0:T(8,128)(2,1)}, u32[]{:S(2)}) copy-start(bf16[8,4096]{1,0:T(8,128)(2,1)} %param.11) | copy-start | bytes 196612
  17.0 41.7 %copy-start.3 = (f32[4096]{0:T(1024)S(1)}, f32[4096]{0:T(1024)}, u32[]{:S(2)}) copy-start(f32[4096]{0:T(1024)} %param.16) | copy-start | bytes 49156
  61.7 114.7 %all-to-all-start.1 = ((bf16[8,4,8,4096]{3,2,1,0:T(8,128)(2,1)}), bf16[8,4,8,4096]{3,2,1,0:T(8,128)(2,1)S(1)}, u32[]{:S(2)}, u32[]{:S(2)}) async-start(bf16[8,4,8,4096]{3,2,1,0:T(8,128)(2,1)} %convolution_convert_fusion.1), calls=%async_computation.1 | async-start | bytes 4194304 | tf_op jit(solution)/shard_map/all_to_all | solution.py:71
  279.2 8.7 %copy-start.4 = (f32[8,8]{1,0:T(8,128)S(1)}, f32[8,8]{1,0:T(8,128)}, u32[]{:S(2)}) copy-start(f32[8,8]{1,0:T(8,128)} %param.18) | copy-start | bytes 772
  279.2 8.9 %copy-start.5 = (s32[8,8]{1,0:T(8,128)S(1)}, s32[8,8]{1,0:T(8,128)}, u32[]{:S(2)}) copy-start(s32[8,8]{1,0:T(8,128)} %param.17) | copy-start | bytes 772
  279.2 88.7 %copy-start.1 = (bf16[2,4,64,128]{3,2,1,0:T(8,128)(2,1)S(1)}, bf16[2,4,64,128]{3,2,1,0:T(8,128)(2,1)}, u32[]{:S(2)}) copy-start(bf16[2,4,64,128]{3,2,1,0:T(8,128)(2,1)} %param.14) | copy-start | bytes 393220
  281.7 55.2 %copy-start.6 = (u32[32]{0:T(128)S(1)}, u32[32]{0:T(128)}, u32[]{:S(2)}) copy-start(u32[32]{0:T(128)} %constant.60) | copy-start | bytes 388
  281.7 52.9 %all-to-all-start.2 = ((bf16[8,4,8,4096]{3,2,1,0:T(8,128)(2,1)}), bf16[8,4,8,4096]{3,2,1,0:T(8,128)(2,1)S(1)}, u32[]{:S(2)}, u32[]{:S(2)}) async-start(bf16[8,4,8,4096]{3,2,1,0:T(8,128)(2,1)} %copy.38), calls=%async_computation.2 | async-start | bytes 4194304 | tf_op jit(solution)/shard_map/all_to_all | solution.py:75
  287.9 78.6 %all-reduce.6.cloned.1.call-start = ((), (), s32[]{:S(2)}) async-start(), calls=%async_computation.4 | async-start | bytes 131072
Sparse Core Ops, SparseCore 0:
  25.9 31.8 all-reduce.3
  337.1 29.3 all-reduce.5
where the time goes:
time: 377 us; the launch traced here: 375 us
  matrix products  118 us (31%)
  local copies, waits for them, and re-layouts  113 us (30%)
  waiting for transfers between devices  110 us (29%)
  starting transfers between devices  15.9 us (4%)
  between operations  14.4 us (4%)
  other arithmetic  3.89 us (1%)
    reshape x1, local copies, waits for them, and re-layouts, shards(): gate_local = w_gate.reshape(d_model, exp_local, slice_width)  54.6 us
    reshape x1, local copies, waits for them, and re-layouts, shards(): up_local = w_up.reshape(d_model, exp_local, slice_width)  54.6 us
    dot_general x1, matrix products, shards(): jnp.einsum('qjkd,dje->qjke', arrived, up_local, preferred_element_type=jn...  49.9 us
    all_to_all x1, waiting for transfers between devices, shards(): lax.all_to_all(jnp.einsum('qjke,jed->qjkd', act, down_local, preferred_el...  46.3 us
    dot_general x1, matrix products, shards(): jnp.einsum('qjkd,dje->qjke', arrived, gate_local, preferred_element_type=...  39.1 us
    psum x1, waiting for transfers between devices, shards(): attn = lax.psum(partial_sum.astype(jnp.bfloat16), 'col').astype(jnp.float32)  31.8 us
    unnamed x3, waiting for transfers between devices  28.3 us
    dot_general x1, matrix products, shards(): jnp.einsum('qjke,jed->qjkd', act, down_local, preferred_element_type=jnp....  13.8 us
  transfers between devices with their start and end apart: 5, of which 4 were waited for; matrix products, arithmetic and copies ran while one was open for 30% of the time, Pallas kernels for 0%

commit v1 on v0

--- a/solution.py
+++ b/solution.py
@@ -12,6 +12,11 @@
 def normalize(resid, norm_gain):
     mean_square = jnp.mean(resid * resid, axis=-1, keepdims=True)
     return (resid * lax.rsqrt(mean_square + 1e-06) * norm_gain).astype(jnp.bfloat16)
+
+
+def gather(block, axis, count):
+    copies = jnp.broadcast_to(block[None], (count,) + block.shape)
+    return lax.all_to_all(copies, axis, split_axis=0, concat_axis=0, tiled=True)
 
 
 def shards(
@@ -38,10 +43,6 @@
     context = context.astype(jnp.bfloat16).reshape(tok_dev, heads * head_dim)
     head_rows = lax.all_to_all(context, "col", split_axis=1, concat_axis=0, tiled=True)
     partial_sum = jnp.dot(head_rows, out_proj, preferred_element_type=jnp.float32)
-    attn = lax.psum(partial_sum.astype(jnp.bfloat16), "col").astype(jnp.float32)
-    row_resid = hidden.astype(jnp.float32) + attn
-    normed = normalize(row_resid, norm_gain)
-    resid = lax.dynamic_slice_in_dim(row_resid, col_id * tok_dev, tok_dev, 0)
     route_weight = (route_probs / jnp.sum(route_probs, axis=-1, keepdims=True)).astype(jnp.bfloat16)
     exp_local = max(1, hid_dev // FF)
     slice_width = hid_dev // exp_local
@@ -53,6 +54,42 @@
     chosen = jnp.sum(
         jnp.where(match, route_weight[:, :, None, None], jnp.zeros((), jnp.bfloat16)), axis=1
     )
+    if routes.shape[0] <= CAP:
+        spread = lax.all_to_all(
+            jnp.transpose(chosen, (1, 0, 2)).astype(jnp.float32),
+            "row", split_axis=0, concat_axis=0, tiled=True,
+        )
+        spread = spread.reshape(row_count, col_count, tok_dev, exp_local)
+        spread = jnp.transpose(spread, (1, 0, 2, 3)).reshape(-1, exp_local)
+        parts = partial_sum.astype(jnp.bfloat16).reshape(col_count, tok_dev, d_model)
+        parts = lax.all_to_all(parts, "col", split_axis=0, concat_axis=0, tiled=True)
+        attn = jnp.sum(parts.astype(jnp.float32), axis=0)
+        own = lax.dynamic_slice_in_dim(hidden, col_id * tok_dev, tok_dev, 0)
+        resid = own.astype(jnp.float32) + attn
+        normed = normalize(resid, norm_gain)
+        normed = gather(gather(normed, "row", row_count).reshape(-1, d_model), "col", col_count)
+        normed = normed.reshape(-1, d_model)
+        gate = jnp.dot(normed, w_gate, preferred_element_type=jnp.float32)
+        upward = jnp.dot(normed, w_up, preferred_element_type=jnp.float32)
+        widen = jnp.arange(exp_local)[:, None] == jnp.arange(hid_dev)[None, :] // slice_width
+        scale = jnp.dot(
+            spread.astype(jnp.bfloat16),
+            widen.astype(jnp.bfloat16),
+            preferred_element_type=jnp.float32,
+        )
+        act = (jax.nn.silu(gate) * upward * scale).astype(jnp.bfloat16)
+        down = jnp.dot(act, w_down, preferred_element_type=jnp.float32).astype(jnp.bfloat16)
+        down = down.reshape(col_count, -1, d_model)
+        down = lax.all_to_all(down, "col", split_axis=0, concat_axis=0, tiled=True)
+        down = jnp.sum(down.astype(jnp.float32), axis=0).astype(jnp.bfloat16)
+        down = down.reshape(row_count, tok_dev, d_model)
+        down = lax.all_to_all(down, "row", split_axis=0, concat_axis=0, tiled=True)
+        mixture = jnp.sum(down.astype(jnp.float32), axis=0)
+        return (resid + mixture).astype(jnp.bfloat16)
+    attn = lax.psum(partial_sum.astype(jnp.bfloat16), "col").astype(jnp.float32)
+    row_resid = hidden.astype(jnp.float32) + attn
+    normed = normalize(row_resid, norm_gain)
+    resid = lax.dynamic_slice_in_dim(row_resid, col_id * tok_dev, tok_dev, 0)
     before = jnp.cumsum(hits, axis=0) - hits
     hits_t = jnp.transpose(hits, (1, 2, 0))
     before_t = jnp.transpose(before, (1, 2, 0))

time: 377 us -> 128 us (0.34)
  local copies, waits for them, and re-layouts: 113 us -> 3.98 us
  waiting for transfers between devices: 110 us -> 26.9 us
  matrix products: 118 us -> 47.7 us
  blocking collectives: 0 us -> 21 us
  between operations: 14.4 us -> 0.13 us
  starting transfers between devices: 15.9 us -> 20.6 us
    reshape x2, local copies, waits for them, and re-layouts: 109 us -> 0.79 us  [the longest x1 0.69 us: shards(): partial_sum.astype(jnp.bfloat16).reshape(col_count, tok_dev, d_model)]
    dot_general x5 -> x3, matrix products: 108 us -> 38.3 us  [the longest x1 24.4 us: shards(): jnp.dot(act, w_down, preferred_element_type=jnp.float32)]
    psum x1 -> x0, waiting for transfers between devices: 31.8 us -> none  [shards(): attn = lax.psum(partial_sum.astype(jnp.bfloat16), 'col').astype(jnp.float32)]
    unnamed x3 -> x0, waiting for transfers between devices: 28.3 us -> none
    all_to_all x2 -> x4, waiting for transfers between devices: 46.3 us -> 24.6 us  [the longest x2 14.1 us: gather(): return lax.all_to_all(copies, axis, split_axis=0, concat_axis=0, tiled=True)]
    all_to_all x0 -> x2, blocking collectives: none -> 21 us  [the longest x1 11.2 us: shards(): down = lax.all_to_all(down, 'col', split_axis=0, concat_axis=0, tiled=True)]
    all_to_all x2 -> x4, starting transfers between devices: 11.6 us -> 16.4 us  [the longest x2 9.78 us: gather(): return lax.all_to_all(copies, axis, split_axis=0, concat_axis=0, tiled=True)]
  transfers between devices with their start and end apart: 5 -> 5, of which waited for: 4 -> 5; matrix products, arithmetic and copies ran while one was open for 30% -> 3% of each run, Pallas kernels for 0% -> 0%
where the time goes in v1:
time: 128 us; the launch traced here: 127 us
  matrix products  47.7 us (37%)
  waiting for transfers between devices  26.9 us (21%)
  blocking collectives  21 us (16%)
  starting transfers between devices  20.6 us (16%)
  other arithmetic  6.33 us (5%)
  local copies, waits for them, and re-layouts  3.98 us (3%)
    dot_general x1, matrix products, shards(): jnp.dot(act, w_down, preferred_element_type=jnp.float32)  24.4 us
    all_to_all x2, waiting for transfers between devices, gather(): return lax.all_to_all(copies, axis, split_axis=0, concat_axis=0, tiled=True)  14.1 us
    dot_general x1, matrix products, shards(): gate = jnp.dot(normed, w_gate, preferred_element_type=jnp.float32)  13.6 us
    all_to_all x1, blocking collectives, shards(): down = lax.all_to_all(down, 'col', split_axis=0, concat_axis=0, tiled=True)  11.2 us
    all_to_all x2, starting transfers between devices, gather(): return lax.all_to_all(copies, axis, split_axis=0, concat_axis=0, tiled=True)  9.78 us
    all_to_all x1, blocking collectives, shards(): down = lax.all_to_all(down, 'row', split_axis=0, concat_axis=0, tiled=True)  9.74 us
    dot_general x1, matrix products, shards(): jnp.dot(head_rows, out_proj, preferred_element_type=jnp.float32)  8.04 us
    all_to_all x1, waiting for transfers between devices, shards(): lax.all_to_all(jnp.transpose(chosen, (1, 0, 2)).astype(jnp.float32), 'row...  6.39 us
  transfers between devices with their start and end apart: 5, of which 5 were waited for; matrix products, arithmetic and copies ran while one was open for 3% of the time, Pallas kernels for 0%

profile of v1, /device:TPU:0, one launch (start us, length us, event | category | flops | bytes accessed | tf_op | source)
XLA Modules:
  0.0 126.7 jit_solution(12937922747454646763)
XLA Ops:
  0.0 1.1 convolution_multiply_fusion.1
  1.1 0.2 fusion.20
  1.3 0.3 convolution_convert_fusion.2
  1.7 0.6 copy.32
  2.3 4.2 %all-to-all-start = ((bf16[2,4,2048]{2,0,1:T(2,128)(2,1)}), bf16[2,4,2048]{2,0,1:T(2,128)(2,1)S(1)}, u32[]{:S(2)}, u32[]{:S(2)}) async-start(bf16[2,4,2048]{2,0,1:T(2,128)(2,1)} %copy.32), calls=%async_computation | async-start | bytes 65536 | tf_op jit(solution)/shard_map/all_to_all | solution.py:44
  6.5 0.8 reduce_sum.72
  7.3 0.8 divide_convert_fusion.2
  8.1 2.4 %all-to-all-done = bf16[2,4,2048]{2,0,1:T(2,128)(2,1)S(1)} async-done(((bf16[2,4,2048]{2,0,1:T(2,128)(2,1)}), bf16[2,4,2048]{2,0,1:T(2,128)(2,1)S(1)}, u32[]{:S(2)}, u32[]{:S(2)}) %all-to-all-start) | async-done | bytes 32800 | tf_op jit(solution)/shard_map/all_to_all | solution.py:44
  10.5 8.0 %convolution_convert_fusion.1 = bf16[8,4096]{1,0:T(8,128)(2,1)S(1)} fusion(bf16[8,2048]{1,0:T(8,128)(2,1)S(1)} %all_to_all.35, bf16[2048,4096]{1,0:T(8,128)(2,1)} %param.15), kind=kOutput, calls=%fused_computation.5 | convolution fusion | flops 134250496 | bytes 16875520 | tf_op jit(solution)/shard_map/dot_general | solution.py:45
  18.5 0.7 reshape.139
  19.2 3.3 %all-to-all-start.1 = ((bf16[4,2,4096]{2,1,0:T(2,128)(2,1)}), bf16[4,2,4096]{2,1,0:T(2,128)(2,1)S(1)}, u32[]{:S(2)}, u32[]{:S(2)}) async-start(bf16[4,2,4096]{2,1,0:T(2,128)(2,1)} %reshape.139), calls=%async_computation.1 | async-start | bytes 131072 | tf_op jit(solution)/shard_map/all_to_all | solution.py:65
  22.5 4.1 %all-to-all-done.1 = bf16[4,2,4096]{2,1,0:T(2,128)(2,1)S(1)} async-done(((bf16[4,2,4096]{2,1,0:T(2,128)(2,1)}), bf16[4,2,4096]{2,1,0:T(2,128)(2,1)S(1)}, u32[]{:S(2)}, u32[]{:S(2)}) %all-to-all-start.1) | async-done | bytes 65568 | tf_op jit(solution)/shard_map/all_to_all | solution.py:65
  26.6 1.0 multiply_reduce_fusion
  27.6 0.9 multiply_convert_fusion
  28.6 0.7 broadcast_in_dim.18
  29.3 6.3 %all-to-all-start.2 = ((bf16[8,2,4096]{2,1,0:T(2,128)(2,1)}), bf16[8,2,4096]{2,1,0:T(2,128)(2,1)S(1)}, u32[]{:S(2)}, u32[]{:S(2)}) async-start(bf16[8,2,4096]{2,1,0:T(2,128)(2,1)} %broadcast_in_dim.18), calls=%async_computation.2 | async-start | bytes 262144 | tf_op jit(solution)/shard_map/all_to_all | solution.py:19
  35.6 0.8 fusion.11
  36.4 0.7 copy.33
  37.1 5.8 %all-to-all-done.2 = bf16[8,2,4096]{2,1,0:T(2,128)(2,1)S(1)} async-done(((bf16[8,2,4096]{2,1,0:T(2,128)(2,1)}), bf16[8,2,4096]{2,1,0:T(2,128)(2,1)S(1)}, u32[]{:S(2)}, u32[]{:S(2)}) %all-to-all-start.2) | async-done | bytes 131104 | tf_op jit(solution)/shard_map/all_to_all | solution.py:19
  43.0 3.3 %all-to-all-start.4 = ((bf16[8,8,4]{1,2,0:T(4,128)(2,1)}), bf16[8,8,4]{1,2,0:T(4,128)(2,1)S(1)}, u32[]{:S(2)}, u32[]{:S(2)}) async-start(bf16[8,8,4]{1,2,0:T(4,128)(2,1)} %copy.33), calls=%async_computation.4 | async-start | bytes 16384 | tf_op jit(solution)/shard_map/all_to_all | solution.py:58
  46.4 6.4 %all-to-all-done.4 = bf16[8,8,4]{1,2,0:T(4,128)(2,1)S(1)} async-done(((bf16[8,8,4]{1,2,0:T(4,128)(2,1)}), bf16[8,8,4]{1,2,0:T(4,128)(2,1)S(1)}, u32[]{:S(2)}, u32[]{:S(2)}) %all-to-all-start.4) | async-done | bytes 544 | tf_op jit(solution)/shard_map/all_to_all | solution.py:58
  52.8 0.8 broadcast_in_dim.20
  53.6 3.5 %all-to-all-start.3 = ((bf16[4,16,4096]{2,1,0:T(8,128)(2,1)}), bf16[4,16,4096]{2,1,0:T(8,128)(2,1)S(1)}, u32[]{:S(2)}, u32[]{:S(2)}) async-start(bf16[4,16,4096]{2,1,0:T(8,128)(2,1)} %broadcast_in_dim.20), calls=%async_computation.3 | async-start | bytes 1048576 | tf_op jit(solution)/shard_map/all_to_all | solution.py:19
  57.2 0.1 copy.35
  57.3 0.3 fusion.12
  57.6 8.3 %all-to-all-done.3 = bf16[4,16,4096]{2,1,0:T(8,128)(2,1)S(1)} async-done(((bf16[4,16,4096]{2,1,0:T(8,128)(2,1)}), bf16[4,16,4096]{2,1,0:T(8,128)(2,1)S(1)}, u32[]{:S(2)}, u32[]{:S(2)}) %all-to-all-start.3) | async-done | bytes 524320 | tf_op jit(solution)/shard_map/all_to_all | solution.py:19
  65.9 13.6 %fusion.21 = f32[64,4096]{1,0:T(8,128)S(1)} fusion(bf16[64,4096]{1,0:T(8,128)(2,1)S(1)} %bitcast.26, bf16[4096,4096]{1,0:T(8,128)(2,1)} %param.19), kind=kOutput, calls=%fused_computation.47 | convolution fusion | flops 2147483648 | bytes 35127296 | tf_op jit(solution)/shard_map/dot_general | solution.py:72
  79.5 24.4 %convolution_convert_fusion = bf16[64,4096]{1,0:T(8,128)(2,1)S(1)} fusion(bf16[4096,4096]{1,0:T(8,128)(2,1)} %param.21, f32[64,4096]{1,0:T(8,128)S(1)} %fusion.12, bf16[64,4096]{1,0:T(8,128)(2,1)S(1)} %bitcast.27, bf16[4096,4096]{1,0:T(8,128)(2,1)} %param.20, f32[64,4096]{1,0:T(8,128)S(1)} %fusion.21), kind=kOutput, calls=%fused_computation.4 | convolution fusion | flops 4297064448 | bytes 70254592 | tf_op jit(solution)/shard_map/dot_general | solution.py:81
  103.9 11.2 %all_to_all.49 = bf16[4,16,4096]{2,1,0:T(8,128)(2,1)S(1)} all-to-all(bf16[4,16,4096]{2,1,0:T(8,128)(2,1)S(1)} %bitcast.28), channel_id=1, replica_groups=mesh['row'=8,'col'=4] {'col'}, dimensions={0} | all-to-all | bytes 1048576 | tf_op jit(solution)/shard_map/all_to_all | solution.py:83
  115.3 9.7 %all_to_all.50 = bf16[8,2,4096]{2,1,0:T(2,128)(2,1)S(1)} all-to-all(bf16[8,2,4096]{2,1,0:T(2,128)(2,1)S(1)} %reshape.142), channel_id=1, replica_groups=mesh['row'=8,'col'=4] {'row'}, dimensions={0} | all-to-all | bytes 262144 | tf_op jit(solution)/shard_map/all_to_all | solution.py:86
  125.1 0.2 convert_reduce_fusion
  125.2 1.5 %add_convert_fusion = bf16[2,4096]{1,0:T(2,128)(2,1)} fusion(f32[2,4096]{1,0:T(2,128)S(1)} %convert_reduce_fusion, f32[2,4096]{1,0:T(2,128)S(1)} %convert_reduce_fusion.1, bf16[8,4096]{1,0:T(8,128)(2,1)} %param.11, s32[]{:T(128)S(6)} %select_n.27), kind=kLoop, calls=%fused_computation.23 | loop fusion | flops 32768 | bytes 98308 | tf_op jit(solution)/shard_map/convert_element_type | solution.py:88
  (15 shorter events, 0.5 us)
Async XLA Ops:
  0.0 1.3 %copy-start = (bf16[2,4,64,128]{3,2,1,0:T(8,128)(2,1)S(1)}, bf16[2,4,64,128]{3,2,1,0:T(8,128)(2,1)}, u32[]{:S(2)}) copy-start(bf16[2,4,64,128]{3,2,1,0:T(8,128)(2,1)} %param.14) | copy-start | bytes 393220
  2.3 8.2 %all-to-all-start = ((bf16[2,4,2048]{2,0,1:T(2,128)(2,1)}), bf16[2,4,2048]{2,0,1:T(2,128)(2,1)S(1)}, u32[]{:S(2)}, u32[]{:S(2)}) async-start(bf16[2,4,2048]{2,0,1:T(2,128)(2,1)} %copy.32), calls=%async_computation | async-start | bytes 65536 | tf_op jit(solution)/shard_map/all_to_all | solution.py:44
  19.2 7.4 %all-to-all-start.1 = ((bf16[4,2,4096]{2,1,0:T(2,128)(2,1)}), bf16[4,2,4096]{2,1,0:T(2,128)(2,1)S(1)}, u32[]{:S(2)}, u32[]{:S(2)}) async-start(bf16[4,2,4096]{2,1,0:T(2,128)(2,1)} %reshape.139), calls=%async_computation.1 | async-start | bytes 131072 | tf_op jit(solution)/shard_map/all_to_all | solution.py:65
  29.3 13.7 %all-to-all-start.2 = ((bf16[8,2,4096]{2,1,0:T(2,128)(2,1)}), bf16[8,2,4096]{2,1,0:T(2,128)(2,1)S(1)}, u32[]{:S(2)}, u32[]{:S(2)}) async-start(bf16[8,2,4096]{2,1,0:T(2,128)(2,1)} %broadcast_in_dim.18), calls=%async_computation.2 | async-start | bytes 262144 | tf_op jit(solution)/shard_map/all_to_all | solution.py:19
  43.0 9.8 %all-to-all-start.4 = ((bf16[8,8,4]{1,2,0:T(4,128)(2,1)}), bf16[8,8,4]{1,2,0:T(4,128)(2,1)S(1)}, u32[]{:S(2)}, u32[]{:S(2)}) async-start(bf16[8,8,4]{1,2,0:T(4,128)(2,1)} %copy.33), calls=%async_computation.4 | async-start | bytes 16384 | tf_op jit(solution)/shard_map/all_to_all | solution.py:58
  53.6 12.3 %all-to-all-start.3 = ((bf16[4,16,4096]{2,1,0:T(8,128)(2,1)}), bf16[4,16,4096]{2,1,0:T(8,128)(2,1)S(1)}, u32[]{:S(2)}, u32[]{:S(2)}) async-start(bf16[4,16,4096]{2,1,0:T(8,128)(2,1)} %broadcast_in_dim.20), calls=%async_computation.3 | async-start | bytes 1048576 | tf_op jit(solution)/shard_map/all_to_all | solution.py:19
  65.9 60.8 %copy-start.1 = (bf16[2,4,64,128]{3,2,1,0:T(8,128)(2,1)S(1)}, bf16[2,4,64,128]{3,2,1,0:T(8,128)(2,1)}, u32[]{:S(2)}) copy-start(bf16[2,4,64,128]{3,2,1,0:T(8,128)(2,1)} %param.14) | copy-start | bytes 393220

commit v2 on v1

--- a/solution.py
+++ b/solution.py
@@ -1,12 +1,280 @@
+import functools
 import math
 
 import jax
 import jax.numpy as jnp
 from jax import lax
+from jax.experimental import pallas as pl
+from jax.experimental.pallas import tpu as pltpu
 from jax.sharding import PartitionSpec as P
 
 FF = 1024
 CAP = 8
+WIDTH = 512
+SLOTS = 12
+
+
+def fold(block):
+    half = block.shape[1] // 2
+    return jnp.concatenate([block[:, :half], block[:, half:]], axis=0).astype(jnp.bfloat16)
+
+
+def unfold(block):
+    block = block.astype(jnp.float32)
+    half = block.shape[0] // 2
+    return jnp.concatenate([block[:half], block[half:]], axis=1)
+
+
+def layer(
+    n_row, n_col, heads_ref, hidden_ref, gain_ref, chosen_ref, proj, w_gate, w_up, w_down, out_ref,
+    ring, parts, blocks, picks, wide, normed, act, result, outbox, inbox, final, resid, load_sem,
+    proj_sem, part_sem, block_sem, pick_sem, box_send, box_recv, final_sem,
+):
+    row, col = lax.axis_index("row"), lax.axis_index("col")
+    rows = heads_ref.shape[0]
+    depth = heads_ref.shape[1]
+    model = hidden_ref.shape[1]
+    count = act.shape[1] // WIDTH
+    steps = model // WIDTH
+    per_slot = ring.shape[1] // depth
+    first = steps // per_slot
+
+    def row_peer(off):
+        return (lax.rem(row + off, n_row), col)
+
+    def col_peer(off):
+        return (row, lax.rem(col + off, n_col))
+
+    def send(source, target, sems, off, peer):
+        return pltpu.make_async_remote_copy(
+            src_ref=source, dst_ref=target, send_sem=sems.at[0, off], recv_sem=sems.at[1, off],
+            device_id=peer, device_id_type=pl.DeviceIdType.MESH,
+        )
+
+    def load_proj(j):
+        slot, half = j // per_slot, j % per_slot
+        return pltpu.make_async_copy(
+            proj.at[:, pl.ds(j * WIDTH, WIDTH)],
+            ring.at[slot, pl.ds(half * depth, depth)],
+            proj_sem.at[j],
+        )
+
+    def load(weight, i, at):
+        slot = lax.rem(at, SLOTS)
+        start = pl.multiple_of(i * WIDTH, WIDTH)
+        return pltpu.make_async_copy(
+            weight.at[:, pl.ds(start, WIDTH)], ring.at[slot], load_sem.at[slot]
+        )
+
+    def load_gate(i):
+        return load(w_gate, i, first + 2 * i)
+
+    def load_up(i):
+        return load(w_up, i, first + 2 * i + 1)
+
+    def load_down(j):
+        return load(w_down, j, first + 2 * count + j)
+
+    for j in range(steps):
+        load_proj(j).start()
+    ready = (SLOTS - first) // 2
+    for i in range(ready):
+        load_gate(i).start()
+        load_up(i).start()
+
+    barrier = pltpu.get_barrier_semaphore()
+    for off in range(1, n_row):
+        pl.semaphore_signal(
+            barrier, inc=1, device_id=row_peer(off), device_id_type=pl.DeviceIdType.MESH
+        )
+    for off in range(1, n_col):
+        pl.semaphore_signal(
+            barrier, inc=1, device_id=col_peer(off), device_id_type=pl.DeviceIdType.MESH
+        )
+    pl.semaphore_wait(barrier, n_row + n_col - 2)
+
+    picks[0] = chosen_ref[...]
+    sends = []
+    for off in range(1, n_row):
+        sends.append(send(picks.at[0], picks.at[off], pick_sem, off, row_peer(off)))
+        sends[-1].start()
+
+    for j in range(steps):
+        load_proj(j).wait()
+        slot, half = j // per_slot, j % per_slot
+        resid[:, j * WIDTH : (j + 1) * WIDTH] = jnp.dot(
+            heads_ref[...],
+            ring[slot, half * depth : (half + 1) * depth],
+            preferred_element_type=jnp.float32,
+        )
+    for i in range(ready, SLOTS // 2):
+        load_gate(i).start()
+        load_up(i).start()
+    parts[0] = fold(resid[...])
+    copies = []
+    for off in range(1, n_col):
+        copies.append(send(parts.at[0], parts.at[off], part_sem, off, col_peer(off)))
+        copies[-1].start()
+    sends += copies
+    for copy in copies:
+        copy.wait_recv()
+    total = unfold(parts[0])
+    for off in range(1, n_col):
+        total = total + unfold(parts[off])
+    total = total + hidden_ref[...].astype(jnp.float32)
+    resid[...] = total
+    scaled = total * lax.rsqrt(jnp.mean(total * total, axis=-1, keepdims=True) + 1e-06)
+    blocks[0] = fold(scaled * gain_ref[...])
+    copies = []
+    for off in range(1, n_row):
+        copies.append(send(blocks.at[0], blocks.at[off], block_sem, off, row_peer(off)))
+        copies[-1].start()
+    for copy in sends[: n_row - 1]:
+        copy.wait_recv()
+    sends += copies
+    for off in range(n_row):
+        if off:
+            copies[off - 1].wait_recv()
+        origin = lax.rem(row + n_row - off, n_row)
+        wide[pl.ds(pl.multiple_of(origin * rows, rows), rows), :] = unfold(blocks[off])
+    normed[...] = wide[...].astype(jnp.bfloat16)
+    experts = picks.shape[2]
+    weights = wide.at[:, pl.ds(0, experts)]
+    for off in range(n_row):
+        origin = lax.rem(row + n_row - off, n_row)
+        weights[pl.ds(pl.multiple_of(origin * rows, rows), rows), :] = picks[off]
+
+    def expert_step(i):
+        load_gate(i).wait()
+        gate = jnp.dot(
+            normed[...], ring[lax.rem(first + 2 * i, SLOTS)], preferred_element_type=jnp.float32
+        )
+        load_up(i).wait()
+        upward = jnp.dot(
+            normed[...], ring[lax.rem(first + 2 * i + 1, SLOTS)], preferred_element_type=jnp.float32
+        )
+        expert = ((row * n_col + col) * act.shape[1] + i * WIDTH) // FF
+        lane = lax.broadcasted_iota(jnp.int32, (wide.shape[0], experts), 1)
+        scale = jnp.sum(
+            jnp.where(lane == expert, wide[:, :experts], 0.0), axis=1, keepdims=True
+        )
+        value = gate / (1.0 + jnp.exp(-gate)) * upward * scale
+        act[:, pl.ds(pl.multiple_of(i * WIDTH, WIDTH), WIDTH)] = value.astype(jnp.bfloat16)
+
+    middle = count - SLOTS // 2
+    last = (2 * count + steps - SLOTS) // 2
+
+    @pl.loop(0, middle)
+    def _(i):
+        expert_step(i)
+        load_gate(i + SLOTS // 2).start()
+        load_up(i + SLOTS // 2).start()
+
+    @pl.loop(middle, last)
+    def _(i):
+        expert_step(i)
+        load_down(2 * (i - middle)).start()
+        load_down(2 * (i - middle) + 1).start()
+
+    @pl.loop(last, count)
+    def _(i):
+        expert_step(i)
+
+    def box(off, j):
+        return pltpu.make_async_remote_copy(
+            src_ref=outbox.at[off, j], dst_ref=inbox.at[off, j],
+            send_sem=box_send.at[off, j], recv_sem=box_recv.at[off, j],
+            device_id=row_peer(off), device_id_type=pl.DeviceIdType.MESH,
+        )
+
+    @pl.loop(0, steps)
+    def _(j):
+        load_down(j).wait()
+        result[...] = jnp.dot(
+            act[...],
+            ring[lax.rem(first + 2 * count + j, SLOTS)],
+            preferred_element_type=jnp.float32,
+        )
+        for off in range(n_row):
+            target = lax.rem(row + off, n_row)
+            block = fold(result[pl.ds(pl.multiple_of(target * rows, rows), rows), :])
+            if off:
+                outbox[off, j] = block
+                box(off, j).start()
+            else:
+                inbox[0, j] = block
+
+    for j in range(steps):
+        total = unfold(inbox[0, j])
+        for off in range(1, n_row):
+            box(off, j).wait_recv()
+            total = total + unfold(inbox[off, j])
+        wide[0:rows, j * WIDTH : (j + 1) * WIDTH] = total
+    final[0] = fold(wide[0:rows, :])
+    copies = []
+    for off in range(1, n_col):
+        copies.append(send(final.at[0], final.at[off], final_sem, off, col_peer(off)))
+        copies[-1].start()
+    sends += copies
+    total = resid[...] + unfold(final[0])
+    for off in range(1, n_col):
+        copies[off - 1].wait_recv()
+        total = total + unfold(final[off])
+    out_ref[...] = total
+    for copy in sends:
+        copy.wait_send()
+    for off in range(1, n_row):
+        for j in range(steps):
+            box(off, j).wait_send()
+
+
+def fused(head_rows, hidden, norm_gain, chosen, proj, w_gate, w_up, w_down, n_row, n_col):
+    rows, model = hidden.shape
+    tokens = rows * n_row
+    hid = w_gate.shape[1]
+    steps = model // WIDTH
+    experts = chosen.shape[1]
+    vmem = pl.BlockSpec(memory_space=pltpu.VMEM)
+    far = pl.BlockSpec(memory_space=pl.ANY)
+    bf16, f32 = jnp.bfloat16, jnp.float32
+    dma = pltpu.SemaphoreType.DMA
+    flat = (2 * rows, model // 2)
+    mini = (2 * rows, WIDTH // 2)
+    weight_bytes = 2 * (proj.size + w_gate.size + w_up.size + w_down.size)
+    return pl.pallas_call(
+        functools.partial(layer, n_row, n_col),
+        out_shape=jax.ShapeDtypeStruct((rows, model), f32),
+        in_specs=[vmem] * 4 + [far] * 4,
+        out_specs=vmem,
+        scratch_shapes=[
+            pltpu.VMEM((SLOTS, model, WIDTH), bf16),
+            pltpu.VMEM((n_col,) + flat, bf16),
+            pltpu.VMEM((n_row,) + flat, bf16),
+            pltpu.VMEM((n_row, rows, experts), f32),
+            pltpu.VMEM((tokens, model), f32),
+            pltpu.VMEM((tokens, model), bf16),
+            pltpu.VMEM((tokens, hid), bf16),
+            pltpu.VMEM((tokens, WIDTH), f32),
+            pltpu.VMEM((n_row, steps) + mini, bf16),
+            pltpu.VMEM((n_row, steps) + mini, bf16),
+            pltpu.VMEM((n_col,) + flat, bf16),
+            pltpu.VMEM((rows, model), f32),
+            dma((SLOTS,)),
+            dma((steps,)),
+            dma((2, n_col)),
+            dma((2, n_row)),
+            dma((2, n_row)),
+            dma((n_row, steps)),
+            dma((n_row, steps)),
+            dma((2, n_col)),
+        ],
+        compiler_params=pltpu.CompilerParams(
+            collective_id=0, has_side_effects=True, vmem_limit_bytes=60 * 2**20
+        ),
+        cost_estimate=pl.CostEstimate(
+            flops=tokens * weight_bytes, bytes_accessed=weight_bytes, transcendentals=tokens * hid
+        ),
+    )(head_rows, hidden, norm_gain, chosen, proj, w_gate, w_up, w_down)
 
 
 def normalize(resid, norm_gain):
@@ -42,6 +310,19 @@
     )
     context = context.astype(jnp.bfloat16).reshape(tok_dev, heads * head_dim)
     head_rows = lax.all_to_all(context, "col", split_axis=1, concat_axis=0, tiled=True)
+    experts = hid_dev * row_count * col_count // FF
+    slots_fit = d_model == hid_dev and d_model == 2 * head_rows.shape[1]
+    if routes.shape[0] == CAP and slots_fit and experts % 128 == 0 and hid_dev == 8 * WIDTH:
+        share = route_probs / jnp.sum(route_probs, axis=-1, keepdims=True)
+        share = share.astype(jnp.bfloat16).astype(jnp.float32)
+        chosen = jnp.sum(
+            jnp.where(routes[:, :, None] == jnp.arange(experts), share[:, :, None], 0.0), axis=1
+        )
+        total = fused(
+            head_rows, hidden, norm_gain[None], chosen, out_proj, w_gate, w_up, w_down,
+            row_count, col_count,
+        )
+        return lax.dynamic_slice_in_dim(total, col_id * tok_dev, tok_dev, 0).astype(jnp.bfloat16)
     partial_sum = jnp.dot(head_rows, out_proj, preferred_element_type=jnp.float32)
     route_weight = (route_probs / jnp.sum(route_probs, axis=-1, keepdims=True)).astype(jnp.bfloat16)
     exp_local = max(1, hid_dev // FF)

time: 128 us -> 72.2 us (0.56)
  Pallas kernels: 0 us -> 59.2 us
  matrix products: 47.7 us -> 1.41 us
  waiting for transfers between devices: 26.9 us -> 1.01 us
  blocking collectives: 21 us -> 0 us
  starting transfers between devices: 20.6 us -> 4.21 us
  other arithmetic: 6.33 us -> 3.14 us
    pallas_call x0 -> x1, Pallas kernels: none -> 59.2 us  [fused(): pl.pallas_call(functools.partial(layer, n_row, n_col), out_shape=jax.Shap...]
    dot_general x4 -> x0, matrix products: 46.3 us -> none  [the longest x1 24.4 us: shards(): jnp.dot(act, w_down, preferred_element_type=jnp.float32)]
    all_to_all x4 -> x0, waiting for transfers between devices: 24.6 us -> none  [the longest x2 14.1 us: gather(): return lax.all_to_all(copies, axis, split_axis=0, concat_axis=0, tiled=True)]
    all_to_all x2 -> x0, blocking collectives: 21 us -> none  [the longest x1 11.2 us: shards(): down = lax.all_to_all(down, 'col', split_axis=0, concat_axis=0, tiled=True)]
    all_to_all x4 -> x0, starting transfers between devices: 16.4 us -> none  [the longest x2 9.78 us: gather(): return lax.all_to_all(copies, axis, split_axis=0, concat_axis=0, tiled=True)]
    convert_element_type x3 -> x1, other arithmetic: 3.19 us -> 0.76 us  [shards(): share = share.astype(jnp.bfloat16).astype(jnp.float32)]
    broadcast_in_dim x3 -> x0, local copies, waits for them, and re-layouts: 1.58 us -> none  [gather(): copies = jnp.broadcast_to(block[None], (count,) + block.shape)]
    all_to_all x1, waiting for transfers between devices: 2.38 us -> 1.01 us  [shards(): lax.all_to_all(context, 'col', split_axis=1, concat_axis=0, tiled=True)]
  transfers between devices with their start and end apart: 5 -> 1, of which waited for: 5 -> 1; matrix products, arithmetic and copies ran while one was open for 3% -> 4% of each run, Pallas kernels for 0% -> 0%
where the time goes in v2:
time: 72.2 us; the launch traced here: 71.8 us
  Pallas kernels  59.2 us (82%)
  starting transfers between devices  4.21 us (6%)
  other arithmetic  3.14 us (4%)
  local copies, waits for them, and re-layouts  2.82 us (4%)
  matrix products  1.41 us (2%)
  waiting for transfers between devices  1.01 us (1%)
    pallas_call x1, Pallas kernels, fused(): pl.pallas_call(functools.partial(layer, n_row, n_col), out_shape=jax.Shap...  59.2 us
    all_to_all x1, starting transfers between devices, shards(): lax.all_to_all(context, 'col', split_axis=1, concat_axis=0, tiled=True)  4.21 us
    convert_element_type x1, local copies, waits for them, and re-layouts, shards(): lax.dynamic_slice_in_dim(total, col_id * tok_dev, tok_dev, 0)  1.53 us
  transfers between devices with their start and end apart: 1, of which 1 were waited for; matrix products, arithmetic and copies ran while one was open for 4% of the time, Pallas kernels for 0%

profile of v2, /device:TPU:0, one launch (start us, length us, event | category | flops | bytes accessed | tf_op | source)
XLA Modules:
  0.0 71.8 jit_solution(4353264813368800198)
XLA Ops:
  0.0 0.0 copy-start
  0.0 1.1 %convolution_multiply_fusion = f32[2,4,16,64]{3,2,1,0:T(8,128)S(1)} fusion(bf16[2,4,16,128]{3,2,1,0:T(8,128)(2,1)} %bitcast.11, bf16[2,4,64,128]{3,2,1,0:T(8,128)(2,1)} %param.13), kind=kOutput, calls=%fused_computation.3 | convolution fusion | flops 2105344 | bytes 196608 | tf_op jit(solution)/shard_map/tgqd,tgpd->tgqp/dot_general | solution.py:304
  1.1 0.2 fusion.6
  1.3 0.0 copy-done
  1.3 0.3 convolution_convert_fusion
  1.7 0.6 copy.13
  2.3 4.2 %all-to-all-start = ((bf16[2,4,2048]{2,0,1:T(2,128)(2,1)}), bf16[2,4,2048]{2,0,1:T(2,128)(2,1)S(1)}, u32[]{:S(2)}, u32[]{:S(2)}) async-start(bf16[2,4,2048]{2,0,1:T(2,128)(2,1)} %copy.13), calls=%async_computation | async-start | bytes 65536 | tf_op jit(solution)/shard_map/all_to_all | solution.py:312
  6.5 0.8 %reduce_sum.28 = f32[8]{0:T(128)S(1)} reduce(f32[8,8]{1,0:T(8,128)} %param.18, f32[]{:T(128)} %constant.2.clone.1), dimensions={1}, to_apply=%region_2.0 | reduce | flops 56 | bytes 292 | tf_op jit(solution)/shard_map/reduce_sum | solution.py:316
  7.3 0.8 %fusion.4 = f32[8,8]{1,0:T(8,128)S(1)} fusion(f32[8,8]{1,0:T(8,128)} %param.18, f32[8]{0:T(128)S(1)} %reduce_sum.28), kind=kLoop, calls=%fused_computation.11 | loop fusion | flops 192 | bytes 544 | tf_op jit(solution)/shard_map/convert_element_type | solution.py:317
  8.1 1.4 %select_reduce_fusion.chosen_ref = f32[8,128]{1,0:T(8,128)} fusion(f32[8,8]{1,0:T(8,128)S(1)} %fusion.4, s32[8,8]{1,0:T(8,128)} %param.17), kind=kLoop, calls=%fused_computation.7 | loop fusion | flops 23552 | bytes 4608 | tf_op jit(solution)/shard_map/reduce_sum | solution.py:318
  9.4 1.0 %all-to-all-done = bf16[2,4,2048]{2,0,1:T(2,128)(2,1)S(1)} async-done(((bf16[2,4,2048]{2,0,1:T(2,128)(2,1)}), bf16[2,4,2048]{2,0,1:T(2,128)(2,1)S(1)}, u32[]{:S(2)}, u32[]{:S(2)}) %all-to-all-start) | async-done | bytes 32800 | tf_op jit(solution)/shard_map/all_to_all | solution.py:312
  10.5 0.6 all_to_all.17.heads_ref
  11.1 59.2 %shard_map.109 = f32[8,4096]{1,0:T(8,128)} custom-call(bf16[8,2048]{1,0:T(8,128)(2,1)} %all_to_all.17.heads_ref, bf16[8,4096]{1,0:T(8,128)(2,1)} %hidden_ref.1, f32[1,4096]{1,0:T(1,128)} %bitcast.12, f32[8,128]{1,0:T(8,128)} %select_reduce_fusion.chosen_ref, bf16[2048,4096]{1,0:T(8,128)(2,1)} %proj.1, bf16[4096,4096]{1,0:T(8,128)(2,1)} %w_gate.1, ...), custom_call_target="tpu_custom_call" | custom-call | flops 7516192768 | bytes 117440512 | tf_op jit(solution)/shard_map/pallas_call | solution.py:244
  70.3 1.5 %dynamic-slice_convert_fusion = bf16[2,4096]{1,0:T(2,128)(2,1)} fusion(f32[8,4096]{1,0:T(8,128)} %shard_map.109, s32[]{:T(128)S(6)} %select_n.8), kind=kLoop, calls=%fused_computation.6 | loop fusion | bytes 32772 | tf_op jit(solution)/shard_map/convert_element_type | solution.py:325
  (1 shorter events, 0.0 us)
Async XLA Ops:
  0.0 1.3 %copy-start = (bf16[2,4,64,128]{3,2,1,0:T(8,128)(2,1)S(1)}, bf16[2,4,64,128]{3,2,1,0:T(8,128)(2,1)}, u32[]{:S(2)}) copy-start(bf16[2,4,64,128]{3,2,1,0:T(8,128)(2,1)} %param.14) | copy-start | bytes 393220
  2.3 8.2 %all-to-all-start = ((bf16[2,4,2048]{2,0,1:T(2,128)(2,1)}), bf16[2,4,2048]{2,0,1:T(2,128)(2,1)S(1)}, u32[]{:S(2)}, u32[]{:S(2)}) async-start(bf16[2,4,2048]{2,0,1:T(2,128)(2,1)} %copy.13), calls=%async_computation | async-start | bytes 65536 | tf_op jit(solution)/shard_map/all_to_all | solution.py:312

commit v3 on v2

--- a/solution.py
+++ b/solution.py
@@ -26,13 +26,12 @@
 
 
 def layer(
-    n_row, n_col, heads_ref, hidden_ref, gain_ref, chosen_ref, proj, w_gate, w_up, w_down, out_ref,
+    n_row, n_col, experts, context_ref, hidden_ref, gain_ref, routes_ref, probs_ref, proj, w_gate, w_up, w_down, out_ref,
     ring, parts, blocks, picks, wide, normed, act, result, outbox, inbox, final, resid, load_sem,
-    proj_sem, part_sem, block_sem, pick_sem, box_send, box_recv, final_sem,
+    proj_sem, part_sem, block_sem, pick_sem, box_send, box_recv, final_sem, heads_in, heads, heads_sem,
 ):
     row, col = lax.axis_index("row"), lax.axis_index("col")
-    rows = heads_ref.shape[0]
-    depth = heads_ref.shape[1]
+    rows, depth = heads.shape
     model = hidden_ref.shape[1]
     count = act.shape[1] // WIDTH
     steps = model // WIDTH
@@ -93,17 +92,42 @@
         )
     pl.semaphore_wait(barrier, n_row + n_col - 2)
 
-    picks[0] = chosen_ref[...]
+    heads_in[0] = context_ref[col]
+    heads_copies = []
+    for off in range(1, n_col):
+        target = lax.rem(col + off, n_col)
+        heads_copies.append(
+            send(context_ref.at[target], heads_in.at[off], heads_sem, off, col_peer(off))
+        )
+        heads_copies[-1].start()
+    share = probs_ref[...] / jnp.sum(probs_ref[...], axis=-1, keepdims=True)
+    share = share.astype(jnp.bfloat16).astype(jnp.float32)
+    lanes = lax.broadcasted_iota(jnp.int32, (rows, experts), 1)
+    chosen = jnp.zeros((rows, experts), jnp.float32)
+    for i in range(routes_ref.shape[1]):
+        chosen = chosen + jnp.where(lanes == routes_ref[:, i : i + 1], share[:, i : i + 1], 0.0)
+    picks[0] = chosen
     sends = []
     for off in range(1, n_row):
         sends.append(send(picks.at[0], picks.at[off], pick_sem, off, row_peer(off)))
         sends[-1].start()
 
+    for copy in heads_copies:
+        copy.wait_recv()
+    own = rows // n_col
+    piece = heads_in.shape[2]
+    for origin in range(n_col):
+        got = heads_in[lax.rem(col + n_col - origin, n_col)].astype(jnp.float32)
+        for i in range(depth // piece):
+            heads[origin * own : (origin + 1) * own, i * piece : (i + 1) * piece] = got[
+                i * own : (i + 1) * own
+            ]
+    head_rows = heads[...].astype(jnp.bfloat16)
     for j in range(steps):
         load_proj(j).wait()
         slot, half = j // per_slot, j % per_slot
         resid[:, j * WIDTH : (j + 1) * WIDTH] = jnp.dot(
-            heads_ref[...],
+            head_rows,
             ring[slot, half * depth : (half + 1) * depth],
             preferred_element_type=jnp.float32,
         )
@@ -138,7 +162,6 @@
         origin = lax.rem(row + n_row - off, n_row)
         wide[pl.ds(pl.multiple_of(origin * rows, rows), rows), :] = unfold(blocks[off])
     normed[...] = wide[...].astype(jnp.bfloat16)
-    experts = picks.shape[2]
     weights = wide.at[:, pl.ds(0, experts)]
     for off in range(n_row):
         origin = lax.rem(row + n_row - off, n_row)
@@ -221,19 +244,20 @@
         copies[off - 1].wait_recv()
         total = total + unfold(final[off])
     out_ref[...] = total
-    for copy in sends:
+    for copy in sends + heads_copies:
         copy.wait_send()
     for off in range(1, n_row):
         for j in range(steps):
             box(off, j).wait_send()
 
 
-def fused(head_rows, hidden, norm_gain, chosen, proj, w_gate, w_up, w_down, n_row, n_col):
+def fused(
+    context, hidden, norm_gain, routes, probs, experts, proj, w_gate, w_up, w_down, n_row, n_col
+):
     rows, model = hidden.shape
     tokens = rows * n_row
     hid = w_gate.shape[1]
     steps = model // WIDTH
-    experts = chosen.shape[1]
     vmem = pl.BlockSpec(memory_space=pltpu.VMEM)
     far = pl.BlockSpec(memory_space=pl.ANY)
     bf16, f32 = jnp.bfloat16, jnp.float32
@@ -242,9 +266,9 @@
     mini = (2 * rows, WIDTH // 2)
     weight_bytes = 2 * (proj.size + w_gate.size + w_up.size + w_down.size)
     return pl.pallas_call(
-        functools.partial(layer, n_row, n_col),
+        functools.partial(layer, n_row, n_col, experts),
         out_shape=jax.ShapeDtypeStruct((rows, model), f32),
-        in_specs=[vmem] * 4 + [far] * 4,
+        in_specs=[vmem] * 5 + [far] * 4,
         out_specs=vmem,
         scratch_shapes=[
             pltpu.VMEM((SLOTS, model, WIDTH), bf16),
@@ -267,6 +291,9 @@
             dma((n_row, steps)),
             dma((n_row, steps)),
             dma((2, n_col)),
+            pltpu.VMEM(context.shape, bf16),
+            pltpu.VMEM((rows, proj.shape[0]), f32),
+            dma((2, n_col)),
         ],
         compiler_params=pltpu.CompilerParams(
             collective_id=0, has_side_effects=True, vmem_limit_bytes=60 * 2**20
@@ -274,7 +301,7 @@
         cost_estimate=pl.CostEstimate(
             flops=tokens * weight_bytes, bytes_accessed=weight_bytes, transcendentals=tokens * hid
         ),
-    )(head_rows, hidden, norm_gain, chosen, proj, w_gate, w_up, w_down)
+    )(context, hidden, norm_gain, routes, probs, proj, w_gate, w_up, w_down)
 
 
 def normalize(resid, norm_gain):
@@ -309,20 +336,18 @@
         "tgqp,tgpd->tgqd", attn_weights, values, preferred_element_type=jnp.float32
     )
     context = context.astype(jnp.bfloat16).reshape(tok_dev, heads * head_dim)
+    experts = hid_dev * row_count * col_count // FF
+    slots_fit = d_model == hid_dev and d_model == 2 * out_proj.shape[0]
+    if routes.shape[0] == CAP and slots_fit and experts % 128 == 0 and hid_dev == 8 * WIDTH:
+        own = routes.shape[0] // col_count
+        cut = context.reshape(own, col_count, 16 // own, -1)
+        cut = jnp.transpose(cut, (1, 2, 0, 3)).reshape(col_count, 16, -1)
+        total = fused(
+            cut, hidden, norm_gain[None], routes, route_probs, experts, out_proj, w_gate, w_up, w_down,
+            row_count, col_count,
+        )
+        return lax.dynamic_slice_in_dim(total, col_id * tok_dev, tok_dev, 0).astype(jnp.bfloat16)
     head_rows = lax.all_to_all(context, "col", split_axis=1, concat_axis=0, tiled=True)
-    experts = hid_dev * row_count * col_count // FF
-    slots_fit = d_model == hid_dev and d_model == 2 * head_rows.shape[1]
-    if routes.shape[0] == CAP and slots_fit and experts % 128 == 0 and hid_dev == 8 * WIDTH:
-        share = route_probs / jnp.sum(route_probs, axis=-1, keepdims=True)
-        share = share.astype(jnp.bfloat16).astype(jnp.float32)
-        chosen = jnp.sum(
-            jnp.where(routes[:, :, None] == jnp.arange(experts), share[:, :, None], 0.0), axis=1
-        )
-        total = fused(
-            head_rows, hidden, norm_gain[None], chosen, out_proj, w_gate, w_up, w_down,
-            row_count, col_count,
-        )
-        return lax.dynamic_slice_in_dim(total, col_id * tok_dev, tok_dev, 0).astype(jnp.bfloat16)
     partial_sum = jnp.dot(head_rows, out_proj, preferred_element_type=jnp.float32)
     route_weight = (route_probs / jnp.sum(route_probs, axis=-1, keepdims=True)).astype(jnp.bfloat16)
     exp_local = max(1, hid_dev // FF)

time: 72.2 us -> 66.9 us (0.927)
  starting transfers between devices: 4.21 us -> 0 us
  Pallas kernels: 59.2 us -> 62.7 us
  other arithmetic: 3.14 us -> 0.2 us
  waiting for transfers between devices: 1.01 us -> 0 us
    all_to_all x1 -> x0, starting transfers between devices: 4.21 us -> none  [shards(): lax.all_to_all(context, 'col', split_axis=1, concat_axis=0, tiled=True)]
    pallas_call x1, Pallas kernels: 59.2 us -> 62.7 us  [fused(): pl.pallas_call(functools.partial(layer, n_row, n_col, experts), out_shape...]
    reduce_sum x2 -> x0, other arithmetic: 2.18 us -> none  [the longest x1 1.37 us: shards(): jnp.sum(jnp.where(routes[:, :, None] == jnp.arange(experts), share[:, :,...]
    all_to_all x3 -> x0, local copies, waits for them, and re-layouts: 1.28 us -> none  [shards(): lax.all_to_all(context, 'col', split_axis=1, concat_axis=0, tiled=True)]
    all_to_all x1 -> x0, waiting for transfers between devices: 1.01 us -> none  [shards(): lax.all_to_all(context, 'col', split_axis=1, concat_axis=0, tiled=True)]
    convert_element_type x1 -> x0, other arithmetic: 0.76 us -> none  [shards(): share = share.astype(jnp.bfloat16).astype(jnp.float32)]
  transfers between devices with their start and end apart: 1 -> 0, of which waited for: 1 -> 0; matrix products, arithmetic and copies ran while one was open for 4% -> 0% of each run, Pallas kernels for 0% -> 0%
where the time goes in v3:
time: 66.9 us; the launch traced here: 66.6 us
  Pallas kernels  62.7 us (94%)
  local copies, waits for them, and re-layouts  2.22 us (3%)
  matrix products  1.41 us (2%)
    pallas_call x1, Pallas kernels, fused(): pl.pallas_call(functools.partial(layer, n_row, n_col, experts), out_shape...  62.7 us
    convert_element_type x1, local copies, waits for them, and re-layouts, shards(): lax.dynamic_slice_in_dim(total, col_id * tok_dev, tok_dev, 0)  1.53 us

profile of v3, /device:TPU:0, one launch (start us, length us, event | category | flops | bytes accessed | tf_op | source)
XLA Modules:
  0.0 66.6 jit_solution(5609780576527749043)
XLA Ops:
  0.0 0.0 copy-start
  0.0 1.1 %convolution_multiply_fusion = f32[2,4,16,64]{3,2,1,0:T(8,128)S(1)} fusion(bf16[2,4,16,128]{3,2,1,0:T(8,128)(2,1)} %bitcast.13, bf16[2,4,64,128]{3,2,1,0:T(8,128)(2,1)} %param.13), kind=kOutput, calls=%fused_computation.3 | convolution fusion | flops 2105344 | bytes 196608 | tf_op jit(solution)/shard_map/tgqd,tgpd->tgqp/dot_general | solution.py:331
  1.1 0.2 fusion.5
  1.3 0.0 copy-done
  1.3 0.3 convolution_convert_fusion
  1.7 0.6 reshape.9.context_ref
  2.3 62.7 %shard_map.109 = f32[8,4096]{1,0:T(8,128)} custom-call(bf16[4,16,256]{2,1,0:T(8,128)(2,1)} %reshape.9.context_ref, bf16[8,4096]{1,0:T(8,128)(2,1)} %hidden_ref.1, f32[1,4096]{1,0:T(1,128)} %bitcast.14, s32[8,8]{1,0:T(8,128)} %routes_ref.1, f32[8,8]{1,0:T(8,128)} %probs_ref.1, bf16[2048,4096]{1,0:T(8,128)(2,1)} %proj.1, bf16[4096,4096]{1,0:T(8,128)(2,1)} %w_gate.1, ...), custom_call_target="tpu_custom_call" | custom-call | flops 7516192768 | bytes 117440512 | tf_op jit(solution)/shard_map/pallas_call | solution.py:268
  65.1 1.5 %dynamic-slice_convert_fusion = bf16[2,4096]{1,0:T(2,128)(2,1)} fusion(f32[8,4096]{1,0:T(8,128)} %shard_map.109, s32[]{:T(128)S(6)} %select_n.3), kind=kLoop, calls=%fused_computation.7 | loop fusion | bytes 32772 | tf_op jit(solution)/shard_map/convert_element_type | solution.py:349
  (2 shorter events, 0.1 us)
Async XLA Ops:
  0.0 1.3 %copy-start = (bf16[2,4,64,128]{3,2,1,0:T(8,128)(2,1)S(1)}, bf16[2,4,64,128]{3,2,1,0:T(8,128)(2,1)}, u32[]{:S(2)}) copy-start(bf16[2,4,64,128]{3,2,1,0:T(8,128)(2,1)} %param.14) | copy-start | bytes 393220
